TPU v7x, 256 devices: a whole 4x4x8 slice. The times are simulated.
256 devices in a mesh: dp: 16 (over x, y_hi, core), expert: 16 (over y_lo, z).
Axes of the slice: x: 4, y: 4 (y_hi: 2, y_lo: 2; y = y_hi * 2 + y_lo), z: 8, core: 2. Of those that a mesh axis runs over, the one named last changes fastest.
Arguments:
- tokens: bfloat16 [32768, 1024], P(('dp', 'expert')), may hold values from -6 to 6
- expert_ids: int32 [32768, 8], P(('dp', 'expert')), may hold values from 0 to 63, all different within a row; in each aligned block of 128 rows (0 to 127, 128 to 255, ...) at most 24 rows name the same one
- upstream: bfloat16 [32768, 1024], P(('dp', 'expert')), may hold values from -6 to 6
- router_weight: bfloat16 [1024, 64], replicated, may hold values from -0.1875 to 0.1875
- gate_matrix: bfloat16 [64, 384, 1024], P('expert'), may hold values from -0.1875 to 0.1875
- up_matrix: bfloat16 [64, 384, 1024], P('expert'), may hold values from -0.1875 to 0.1875
- down_matrix: bfloat16 [64, 384, 1024], P('expert'), may hold values from -0.3125 to 0.3125
Outputs:
- mixture: bfloat16 [32768, 1024], P(('dp', 'expert'))
- input_grad: bfloat16 [32768, 1024], P(('dp', 'expert'))
- router_grad: float32 [1024, 64], replicated
- gate_grad: float32 [64, 384, 1024], P('expert', 'dp')
- up_grad: float32 [64, 384, 1024], P('expert', 'dp')
- down_grad: float32 [64, 384, 1024], P('expert', 'dp')
Inputs may be any that keep to these rules, and one draw needn't show every extreme that they name: `expert_ids`: each row names 8 different experts. Among the rows of one device no expert is named more than 24 times, a bound that some block reaches.
All inputs are finite; a program needn't handle non-finite values.
Results may differ from a plain program's by a relative error of at most 0.0063.
Values may be sent and summed in bfloat16 or wider, within the bound.
No kernel may reach another device: no remote copies, remote signals or barrier semaphores. Data moves between devices by JAX's collectives and lax.ppermute only.
A program may use at most 320 MiB of HBM per device.

v0:
```python
import jax
import jax.numpy as jnp
from jax import lax
from jax.sharding import PartitionSpec as P


def slot_positions(expert_ids, experts, capacity):
    flat_ids = expert_ids.reshape(-1)
    columns = lax.broadcasted_iota(jnp.int32, (1, experts), 1)
    onehot = (flat_ids[:, None] == columns).astype(jnp.int32)
    ranking = jnp.cumsum(onehot, axis=0) - 1
    slot_numbers = jnp.sum(ranking * onehot, axis=1)
    return flat_ids * capacity + slot_numbers


def slot_sources(positions, total_slots):
    assign_count = positions.shape[0]
    return (
        jnp.full((total_slots,), -1, jnp.int32)
        .at[positions]
        .set(jnp.arange(assign_count, dtype=jnp.int32))
    )


def fill_slots(source_rows, sources, divisor):
    occupied = sources >= 0
    picked = jnp.take(source_rows, jnp.maximum(sources, 0) // divisor, axis=0)
    return jnp.where(occupied[:, None], picked, jnp.zeros_like(picked))


def backward_local(pre_gate, pre_up, logistic, act_grad):
    gate_back = (act_grad * pre_up * logistic * (1.0 + pre_gate * (1.0 - logistic))).astype(
        jnp.bfloat16
    )
    up_back = (act_grad * (pre_gate * logistic)).astype(jnp.bfloat16)
    return (gate_back, up_back)


def body(tokens, expert_ids, upstream, router_weight, gate_matrix, up_matrix, down_matrix):
    tok_rows, model_width = tokens.shape
    per_token = expert_ids.shape[1]
    exp_dev, hidden = (gate_matrix.shape[0], gate_matrix.shape[1])
    expert_peers = lax.axis_size("expert")
    experts = expert_peers * exp_dev
    capacity = tok_rows * per_token * 3 // (2 * experts)
    positions = slot_positions(expert_ids, experts, capacity)
    sources = slot_sources(positions, experts * capacity)
    send_rows = fill_slots(tokens, sources, per_token).reshape(
        expert_peers, exp_dev * capacity, model_width
    )
    recv_rows = lax.all_to_all(send_rows, "expert", split_axis=0, concat_axis=0, tiled=True)
    expert_rows = recv_rows.reshape(expert_peers, exp_dev, capacity, model_width)
    pre_gate = jnp.einsum(
        "secd,efd->secf", expert_rows, gate_matrix, preferred_element_type=jnp.float32
    )
    pre_up = jnp.einsum(
        "secd,efd->secf", expert_rows, up_matrix, preferred_element_type=jnp.float32
    )
    logistic = jax.nn.sigmoid(pre_gate)
    activated = (pre_gate * logistic * pre_up).astype(jnp.bfloat16)
    produced = jnp.einsum(
        "secf,efd->secd", activated, down_matrix, preferred_element_type=jnp.float32
    ).astype(jnp.bfloat16)
    returned = lax.all_to_all(
        produced.reshape(expert_peers, exp_dev * capacity, model_width),
        "expert",
        split_axis=0,
        concat_axis=0,
        tiled=True,
    )
    assign_out = jnp.take(returned.reshape(experts * capacity, model_width), positions, axis=0)
    assign_out = assign_out.reshape(tok_rows, per_token, model_width).astype(jnp.float32)
    logits = jnp.dot(tokens, router_weight, preferred_element_type=jnp.float32)
    chosen = jnp.take_along_axis(logits, expert_ids, axis=1)
    raised = jnp.exp(chosen)
    gate_probs = raised / jnp.sum(raised, axis=1, keepdims=True)
    mixture = jnp.sum(gate_probs[:, :, None] * assign_out, axis=1).astype(jnp.bfloat16)
    cotangent = upstream.astype(jnp.float32)
    prob_grad = jnp.sum(cotangent[:, None, :] * assign_out, axis=2)
    centered = prob_grad - jnp.sum(gate_probs * prob_grad, axis=1, keepdims=True)
    chosen_grad = gate_probs * centered
    expert_cols = lax.broadcasted_iota(jnp.int32, (1, 1, experts), 2)
    logit_grad = jnp.sum(
        jnp.where(expert_ids[:, :, None] == expert_cols, chosen_grad[:, :, None], 0.0), axis=1
    )
    router_part = jnp.dot(tokens.astype(jnp.float32).T, logit_grad, precision=lax.Precision.HIGHEST)
    router_grad = lax.psum(router_part, ("dp", "expert"))
    router_input = jnp.dot(
        logit_grad, router_weight.astype(jnp.float32).T, precision=lax.Precision.HIGHEST
    )
    out_grad = (gate_probs[:, :, None] * cotangent[:, None, :]).astype(jnp.bfloat16)
    out_grad = out_grad.reshape(tok_rows * per_token, model_width)
    send_grad = fill_slots(out_grad, sources, 1).reshape(
        expert_peers, exp_dev * capacity, model_width
    )
    recv_grad = lax.all_to_all(send_grad, "expert", split_axis=0, concat_axis=0, tiled=True)
    grad_rows = recv_grad.reshape(expert_peers, exp_dev, capacity, model_width)
    act_grad = jnp.einsum(
        "secd,efd->secf", grad_rows, down_matrix, preferred_element_type=jnp.float32
    )
    gate_back, up_back = backward_local(pre_gate, pre_up, logistic, act_grad)
    row_grad = (
        jnp.einsum("secf,efd->secd", gate_back, gate_matrix, preferred_element_type=jnp.float32)
        + jnp.einsum("secf,efd->secd", up_back, up_matrix, preferred_element_type=jnp.float32)
    ).astype(jnp.bfloat16)
    returned_grads = lax.all_to_all(
        row_grad.reshape(expert_peers, exp_dev * capacity, model_width),
        "expert",
        split_axis=0,
        concat_axis=0,
        tiled=True,
    )
    per_assign = jnp.take(
        returned_grads.reshape(experts * capacity, model_width), positions, axis=0
    )
    per_assign = per_assign.reshape(tok_rows, per_token, model_width).astype(jnp.float32)
    input_grad = (jnp.sum(per_assign, axis=1) + router_input).astype(jnp.bfloat16)
    full_gate = jnp.einsum(
        "secf,secd->efd", gate_back, expert_rows, preferred_element_type=jnp.float32
    )
    full_up = jnp.einsum("secf,secd->efd", up_back, expert_rows, preferred_element_type=jnp.float32)
    full_down = jnp.einsum(
        "secf,secd->efd", activated, grad_rows, preferred_element_type=jnp.float32
    )
    gate_grad = lax.psum_scatter(full_gate, "dp", scatter_dimension=1, tiled=True)
    up_grad = lax.psum_scatter(full_up, "dp", scatter_dimension=1, tiled=True)
    down_grad = lax.psum_scatter(full_down, "dp", scatter_dimension=1, tiled=True)
    return (mixture, input_grad, router_grad, gate_grad, up_grad, down_grad)


def solution(mesh):
    in_specs = (
        P(("dp", "expert"), None),
        P(("dp", "expert"), None),
        P(("dp", "expert"), None),
        P(),
        P("expert", None, None),
        P("expert", None, None),
        P("expert", None, None),
    )
    out_specs = (
        P(("dp", "expert"), None),
        P(("dp", "expert"), None),
        P(),
        P("expert", "dp", None),
        P("expert", "dp", None),
        P("expert", "dp", None),
    )
    return jax.shard_map(body, mesh=mesh, in_specs=in_specs, out_specs=out_specs, check_vma=False)
```

profile of v0, /device:TPU:2, one launch (start us, length us, event | category | flops | bytes accessed | tf_op | source)
XLA Modules:
  0.0 670.4 jit_solution(13618022292784977458)
XLA Ops:
  10.9 34.2 %reduce-window.6 = s32[64,8,128]{2,1,0:T(8,128)} reduce-window(s32[64,8,128]{2,1,0:T(8,128)} %fusion.43, s32[]{:T(128)} %constant.85.clone.1), window={size=1x1x128 pad=0_0x0_0x127_0}, to_apply=%region_1.2 | reduce-window | flops 8323072 | bytes 524292 | tf_op jit(solution)/shard_map/reduce-window
  45.1 1.8 slice.18
  49.3 4.3 scatter_custom_fusion
  53.8 5.8 gather_fusion
  59.7 2.2 select_select_fusion.1
  61.9 81.5 %all_to_all.20 = bf16[16,96,1024]{2,1,0:T(8,128)(2,1)S(1)} all-to-all(bf16[16,96,1024]{2,1,0:T(8,128)(2,1)S(1)} %select_select_fusion.1), channel_id=1, replica_groups=mesh['dp'=16,'expert'=16] {'expert'}, dimensions={0} | all-to-all | bytes 6291456 | tf_op jit(solution)/shard_map/all_to_all | solution.py:51
  143.4 1.9 fusion.11
  146.4 3.5 fusion.27
  149.9 1.8 convert_bitcast_fusion.1
  151.7 2.1 copy.64
  153.9 4.8 all-to-all-start.1
  160.0 7.0 %gather_fusion.2 = f32[1024]{0:T(1024)S(1)} fusion(f32[128,64]{0,1:T(8,128)S(1)} %fusion.48, s32[1024]{0:T(1024)S(1)} %reshape.214), kind=kCustom, calls=%fused_computation.4 | custom fusion | bytes 16384 | tf_op jit(solution)/shard_map/jit(take_along_axis)/gather | solution.py:74
  167.3 1.8 convert_element_type.63
  169.2 61.6 %all-to-all-done.1 = bf16[16,96,1024]{2,1,0:T(8,128)(2,1)} async-done(((bf16[16,96,1024]{2,1,0:T(8,128)(2,1)}), bf16[16,96,1024]{2,1,0:T(8,128)(2,1)}, u32[]{:S(2)}, u32[]{:S(2)}) %all-to-all-start.1) | async-done | bytes 3145760 | tf_op jit(solution)/shard_map/all_to_all | solution.py:64
  230.8 8.3 %gather_fusion.3 = bf16[1024,1024]{1,0:T(8,128)(2,1)} fusion(bf16[1536,1024]{1,0:T(8,128)(2,1)} %bitcast.17, s32[1024]{0:T(1024)S(1)} %broadcast_clamp_fusion), kind=kCustom, calls=%fused_computation.clone | custom fusion | bytes 4198400 | tf_op jit(solution)/shard_map/jit(_take)/gather | solution.py:71
  239.2 2.5 fusion.3
  242.1 2.7 fusion.2
  244.8 9.6 %gather_fusion.1 = bf16[1536,1024]{1,0:T(8,128)(2,1)} fusion(bf16[1024,1024]{1,0:T(8,128)(2,1)} %fusion.2, s32[2048]{0:T(1024)S(1)} %pad_clamp_fusion), kind=kCustom, calls=%fused_computation.3 | custom fusion | bytes 6297600 | tf_op jit(solution)/shard_map/jit(_take)/gather | solution.py:27
  254.4 3.4 select_select_fusion
  257.8 7.5 %all-to-all-start.2 = ((bf16[16,96,1024]{2,1,0:T(8,128)(2,1)}), bf16[16,96,1024]{2,1,0:T(8,128)(2,1)}, u32[]{:S(2)}, u32[]{:S(2)}) async-start(bf16[16,96,1024]{2,1,0:T(8,128)(2,1)} %select_select_fusion), calls=%async_computation.2 | async-start | bytes 6291456 | tf_op jit(solution)/shard_map/all_to_all | solution.py:96
  266.4 69.4 %all-to-all-done.2 = bf16[16,96,1024]{2,1,0:T(8,128)(2,1)} async-done(((bf16[16,96,1024]{2,1,0:T(8,128)(2,1)}), bf16[16,96,1024]{2,1,0:T(8,128)(2,1)}, u32[]{:S(2)}, u32[]{:S(2)}) %all-to-all-start.2) | async-done | bytes 3145760 | tf_op jit(solution)/shard_map/all_to_all | solution.py:96
  335.8 6.8 %fusion.20 = f32[4,384,1024]{2,1,0:T(8,128)} fusion(bf16[16,4,24,384]{3,2,0,1:T(8,128)(2,1)} %copy-done.7, bf16[16,4,24,1024]{3,2,1,0:T(8,128)(2,1)} %bitcast.21), kind=kOutput, calls=%fused_computation.34 | convolution fusion | flops 1207959552 | bytes 10616832 | tf_op jit(solution)/shard_map/secf,secd->efd/dot_general | solution.py:122
  342.7 6.8 %fusion.25 = (bf16[16,4,24,384]{3,2,0,1:T(8,128)(2,1)S(1)}, bf16[16,4,24,384]{3,2,0,1:T(8,128)(2,1)}) fusion(f32[4,16,24,384]{3,2,1,0:T(8,128)} %get-tuple-element.18, f32[4,16,24,384]{3,2,1,0:T(8,128)} %copy-done.12, bf16[4,384,1024]{2,1,0:T(8,128)(2,1)S(1)} %copy-done, bf16[16,4,24,1024]{3,2,1,0:T(8,128)(2,1)} %bitcast.21), kind=kOutput, calls=%fused_computation.41 | convolution fusion | flops 1215627264 | bytes 13369344 | tf_op jit(solution)/shard_map/secd,efd->secf/dot_general | solution.py:98
  350.6 4.5 convolution_bitcast_fusion.1
  355.4 6.8 %convolution_bitcast_fusion = f32[4,384,1024]{2,1,0:T(8,128)} fusion(bf16[16,4,24,384]{3,2,0,1:T(8,128)(2,1)} %get-tuple-element.14, bf16[16,4,24,1024]{3,2,1,0:T(8,128)(2,1)} %bitcast.146), kind=kOutput, calls=%fused_computation.35 | convolution fusion | flops 1207959552 | bytes 10616832 | tf_op jit(solution)/shard_map/secf,secd->efd/dot_general | solution.py:121
  362.2 4.5 fusion.5
  366.8 1.8 fusion.4
  368.9 81.1 %all_to_all.21 = bf16[16,96,1024]{2,1,0:T(8,128)(2,1)} all-to-all(bf16[16,96,1024]{2,1,0:T(8,128)(2,1)S(1)} %bitcast.141), channel_id=1, replica_groups=mesh['dp'=16,'expert'=16] {'expert'}, dimensions={0} | all-to-all | bytes 6291456 | tf_op jit(solution)/shard_map/all_to_all | solution.py:106
  450.0 8.4 %gather_fusion.4 = bf16[1024,1024]{1,0:T(8,128)(2,1)} fusion(bf16[1536,1024]{1,0:T(8,128)(2,1)} %bitcast.139, s32[1024]{0:T(1024)S(1)} %broadcast_clamp_fusion), kind=kCustom, calls=%fused_computation.1.clone | custom fusion | bytes 4198400 | tf_op jit(solution)/shard_map/jit(_take)/gather | solution.py:113
  458.3 5.2 convert_reduce_fusion
  464.7 101.7 %all-reduce.2.cloned.1.call-done = f32[1024,64]{0,1:T(8,128)} async-done(((f32[1024,64]{0,1:T(8,128)}), f32[1024,64]{0,1:T(8,128)}) %all-reduce.2.cloned.1.call-update) | async-done | bytes 262160 | tf_op jit(solution)/shard_map/psum | solution.py:87
  566.4 94.6 %reduce-scatter.6.cloned.1.call-done = f32[4,24,1024]{2,1,0:T(8,128)} async-done(((f32[4,384,1024]{2,1,0:T(8,128)}), f32[4,24,1024]{2,1,0:T(8,128)}) %reduce-scatter.6.cloned.1.call-update) | async-done | bytes 393232 | tf_op jit(solution)/shard_map/reduce_scatter | solution.py:126
  (78 shorter events, 14.3 us)
Async XLA Ops:
  8.0 141.9 %copy-start = (bf16[4,384,1024]{2,1,0:T(8,128)(2,1)S(1)}, bf16[4,384,1024]{2,1,0:T(8,128)(2,1)}, u32[]{:S(2)}) copy-start(bf16[4,384,1024]{2,1,0:T(8,128)(2,1)} %param.15) | copy-start | bytes 9437188
  8.0 45.8 %copy-start.1 = (bf16[128,1024]{1,0:T(8,128)(2,1)S(1)}, bf16[128,1024]{1,0:T(8,128)(2,1)}, u32[]{:S(2)}) copy-start(bf16[128,1024]{1,0:T(8,128)(2,1)} %param.9) | copy-start | bytes 786436
  61.8 81.5 %copy-start.4 = (bf16[4,384,1024]{2,1,0:T(8,128)(2,1)S(1)}, bf16[4,384,1024]{2,1,0:T(8,128)(2,1)}, u32[]{:S(2)}) copy-start(bf16[4,384,1024]{2,1,0:T(8,128)(2,1)} %param.13) | copy-start | bytes 9437188
  143.4 1.9 copy-start.2
  143.4 3.0 copy-start.6
  146.4 3.5 copy-start.12
  149.9 1.8 copy-start.7
  153.9 4.8 copy-start.11
  153.9 76.9 %all-to-all-start.1 = ((bf16[16,96,1024]{2,1,0:T(8,128)(2,1)}), bf16[16,96,1024]{2,1,0:T(8,128)(2,1)}, u32[]{:S(2)}, u32[]{:S(2)}) async-start(bf16[16,96,1024]{2,1,0:T(8,128)(2,1)} %bitcast.140), calls=%async_computation.1 | async-start | bytes 6291456 | tf_op jit(solution)/shard_map/all_to_all | solution.py:64
  257.8 78.0 %all-to-all-start.2 = ((bf16[16,96,1024]{2,1,0:T(8,128)(2,1)}), bf16[16,96,1024]{2,1,0:T(8,128)(2,1)}, u32[]{:S(2)}, u32[]{:S(2)}) async-start(bf16[16,96,1024]{2,1,0:T(8,128)(2,1)} %select_select_fusion), calls=%async_computation.2 | async-start | bytes 6291456 | tf_op jit(solution)/shard_map/all_to_all | solution.py:96
  265.2 301.2 %all-reduce.2.cloned.1.call-start = ((), (), s32[]{:S(2)}) async-start(), calls=%async_computation.7 | async-start | bytes 524288 | tf_op jit(solution)/shard_map/psum | solution.py:87
  266.3 300.1 %reduce-scatter.8.cloned.1.call-start = ((), (), s32[]{:S(2)}) async-start(), calls=%async_computation.10 | async-start | bytes 6684672 | tf_op jit(solution)/shard_map/reduce_scatter | solution.py:127
  342.6 223.9 %reduce-scatter.4.cloned.1.call-start = ((), (), s32[]{:S(2)}) async-start(), calls=%async_computation.8 | async-start | bytes 6684672 | tf_op jit(solution)/shard_map/reduce_scatter | solution.py:125
  342.6 7.9 %copy-start.3 = (bf16[16,96,1024]{2,1,0:T(8,128)(2,1)S(1)}, bf16[16,96,1024]{2,1,0:T(8,128)(2,1)}, u32[]{:S(2)}) copy-start(bf16[16,96,1024]{2,1,0:T(8,128)(2,1)} %copy-done.2) | copy-start | bytes 9437188
  349.5 1.1 copy-start.8
  355.1 306.0 %reduce-scatter.6.cloned.1.call-start = ((), (), s32[]{:S(2)}) async-start(), calls=%async_computation.9 | async-start | bytes 6684672 | tf_op jit(solution)/shard_map/reduce_scatter | solution.py:126
  362.2 4.6 copy-start.5
  362.2 4.6 copy-start.9
  458.3 5.2 copy-start.10
Sparse Core Ops, SparseCore 0:
  272.1 294.2 all-reduce.1
Sparse Core Ops, SparseCore 1:
  342.7 116.4 reduce-scatter.7
  464.0 96.0 reduce-scatter.3
  565.0 96.1 reduce-scatter.5
where the time goes:
time: 673 us; the launch traced here: 670 us
  waiting for transfers between devices  327 us (49%)
  blocking collectives  163 us (24%)
  local copies, waits for them, and re-layouts  55.1 us (8%)
  other arithmetic  54.9 us (8%)
  matrix products  41.6 us (6%)
  between operations  16 us (2%)
  starting transfers between devices  12.7 us (2%)
    psum x1, waiting for transfers between devices, body(): router_grad = lax.psum(router_part, ('dp', 'expert'))  102 us
    reduce_scatter x1, waiting for transfers between devices, body(): up_grad = lax.psum_scatter(full_up, 'dp', scatter_dimension=1, tiled=True)  94.6 us
    all_to_all x1, blocking collectives, body(): lax.all_to_all(send_rows, 'expert', split_axis=0, concat_axis=0, tiled=True)  81.5 us
    all_to_all x1, blocking collectives, body(): lax.all_to_all(row_grad.reshape(expert_peers, exp_dev * capacity, model_w...  81.1 us
    all_to_all x1, waiting for transfers between devices, body(): lax.all_to_all(send_grad, 'expert', split_axis=0, concat_axis=0, tiled=True)  69.4 us
    all_to_all x1, waiting for transfers between devices, body(): lax.all_to_all(produced.reshape(expert_peers, exp_dev * capacity, model_w...  61.6 us
    another operation x2, other arithmetic  34.2 us
    gather x2, local copies, waits for them, and re-layouts, fill_slots(): picked = jnp.take(source_rows, jnp.maximum(sources, 0) // divisor, axis=0)  15.5 us
  transfers between devices with their start and end apart: 6, of which 4 were waited for; matrix products, arithmetic and copies ran while one was open for 9% of the time, Pallas kernels for 0%

commit v1 on v0

--- a/solution.py
+++ b/solution.py
@@ -84,7 +84,13 @@
         jnp.where(expert_ids[:, :, None] == expert_cols, chosen_grad[:, :, None], 0.0), axis=1
     )
     router_part = jnp.dot(tokens.astype(jnp.float32).T, logit_grad, precision=lax.Precision.HIGHEST)
-    router_grad = lax.psum(router_part, ("dp", "expert"))
+
+    def follow_the_ranges(tile_in, link_axis):
+        u1 = lax.all_gather(tile_in, link_axis)
+        s_next = jnp.sum(u1, axis=0)
+        return s_next
+
+    router_grad = follow_the_ranges(router_part, ("dp", "expert"))
     router_input = jnp.dot(
         logit_grad, router_weight.astype(jnp.float32).T, precision=lax.Precision.HIGHEST
     )

time: 673 us -> 1250 us (1.86)
  the two profiles are of different devices: /device:TPU:2 before, /device:TPU:99 now
where the time goes in v1:
time: 1250 us
  waiting for transfers between devices  744 us (60%)
  blocking collectives  259 us (21%)
  local copies, waits for them, and re-layouts  109 us (9%)
  other arithmetic  75.2 us (6%)
  matrix products  42.4 us (3%)
  between operations  15.9 us (1%)
    all_gather x1, waiting for transfers between devices, follow_the_ranges(): u1 = lax.all_gather(tile_in, link_axis)  683 us
    all_to_all x1, blocking collectives, body(): lax.all_to_all(send_grad, 'expert', split_axis=0, concat_axis=0, tiled=True)  92.9 us
    all_to_all x1, blocking collectives, body(): lax.all_to_all(row_grad.reshape(expert_peers, exp_dev * capacity, model_w...  87.9 us
    all_to_all x1, blocking collectives, body(): lax.all_to_all(send_rows, 'expert', split_axis=0, concat_axis=0, tiled=True)  78.2 us
    unnamed x38, local copies, waits for them, and re-layouts  61.5 us
    all_to_all x1, waiting for transfers between devices, body(): lax.all_to_all(produced.reshape(expert_peers, exp_dev * capacity, model_w...  60.5 us
    another operation x2, other arithmetic  34.2 us
  transfers between devices with their start and end apart: 5, of which 2 were waited for; matrix products, arithmetic and copies ran while one was open for 12% of the time, Pallas kernels for 0%

profile of v1, /device:TPU:99, one launch (start us, length us, event | category | flops | bytes accessed | tf_op | source)
XLA Modules:
  0.0 1251.5 jit_solution(9821530464806672302)
XLA Ops:
  10.9 34.2 %reduce-window.6 = s32[64,8,128]{2,1,0:T(8,128)} reduce-window(s32[64,8,128]{2,1,0:T(8,128)} %fusion.43, s32[]{:T(128)} %constant.85.clone.1), window={size=1x1x128 pad=0_0x0_0x127_0}, to_apply=%region_1.2 | reduce-window | flops 8323072 | bytes 524292 | tf_op jit(solution)/shard_map/reduce-window
  49.3 4.3 scatter_custom_fusion
  53.8 5.8 gather_fusion
  59.7 2.2 select_select_fusion.1
  61.9 78.2 %all_to_all.20 = bf16[16,96,1024]{2,1,0:T(8,128)(2,1)S(1)} all-to-all(bf16[16,96,1024]{2,1,0:T(8,128)(2,1)S(1)} %select_select_fusion.1), channel_id=1, replica_groups=mesh['dp'=16,'expert'=16] {'expert'}, dimensions={0} | all-to-all | bytes 6291456 | tf_op jit(solution)/shard_map/all_to_all | solution.py:51
  140.0 1.9 fusion.11
  143.0 3.5 fusion.27
  146.5 1.8 convert_bitcast_fusion.1
  148.4 2.1 copy.64
  150.5 6.1 all-to-all-start.1
  156.8 1.8 convert_element_type.63
  159.9 7.0 gather_fusion.2
  167.2 60.5 %all-to-all-done.1 = bf16[16,96,1024]{2,1,0:T(8,128)(2,1)} async-done(((bf16[16,96,1024]{2,1,0:T(8,128)(2,1)}), bf16[16,96,1024]{2,1,0:T(8,128)(2,1)}, u32[]{:S(2)}, u32[]{:S(2)}) %all-to-all-start.1) | async-done | bytes 3145760 | tf_op jit(solution)/shard_map/all_to_all | solution.py:64
  227.6 8.3 gather_fusion.3
  236.0 2.5 fusion.3
  240.1 2.6 fusion.2
  242.7 9.6 gather_fusion.1
  252.4 2.2 select_select_fusion
  254.6 92.9 %all_to_all.21 = bf16[16,96,1024]{2,1,0:T(8,128)(2,1)S(1)} all-to-all(bf16[16,96,1024]{2,1,0:T(8,128)(2,1)S(1)} %select_select_fusion), channel_id=1, replica_groups=mesh['dp'=16,'expert'=16] {'expert'}, dimensions={0} | all-to-all | bytes 6291456 | tf_op jit(solution)/shard_map/all_to_all | solution.py:102
  347.5 3.3 fusion.25
  351.9 4.5 convolution_bitcast_fusion.1
  356.4 1.8 copy-done.5
  358.3 5.8 convolution_bitcast_fusion
  364.4 7.1 fusion.5
  371.4 4.5 fusion.20
  376.0 6.9 fusion.4
  383.3 87.9 %all_to_all.22 = bf16[16,96,1024]{2,1,0:T(8,128)(2,1)S(1)} all-to-all(bf16[16,96,1024]{2,1,0:T(8,128)(2,1)S(1)} %bitcast.145), channel_id=1, replica_groups=mesh['dp'=16,'expert'=16] {'expert'}, dimensions={0} | all-to-all | bytes 6291456 | tf_op jit(solution)/shard_map/all_to_all | solution.py:112
  471.2 5.4 gather_fusion.4
  476.6 5.2 convert_reduce_fusion
  482.9 683.1 %all-gather.3.cloned.1.call-done = f32[262144,64]{0,1:T(8,128)} async-done(((f32[1024,64]{0,1:T(8,128)}), f32[262144,64]{0,1:T(8,128)}) %all-gather.3.cloned.1.call-update) | async-done | bytes 67108880 | tf_op jit(solution)/shard_map/all_gather | solution.py:89
  1166.0 56.4 %copy.80 = f32[8,8,256,1024]{3,2,1,0:T(8,128)} copy(f32[8,8,256,1024]{3,1,2,0:T(8,128)} %bitcast.42) | data formatting | bytes 134217728
  1222.4 21.5 %bitcast_reduce_fusion = f32[1024,64]{0,1:T(8,128)} fusion(f32[8,8,256,1024]{3,2,1,0:T(8,128)} %copy.80), kind=kLoop, calls=%fused_computation.6 | loop fusion | flops 16711680 | bytes 67371008 | tf_op jit(solution)/shard_map/reduce_sum | solution.py:90
  (88 shorter events, 14.7 us)
Async XLA Ops:
  8.0 138.5 %copy-start = (bf16[4,384,1024]{2,1,0:T(8,128)(2,1)S(1)}, bf16[4,384,1024]{2,1,0:T(8,128)(2,1)}, u32[]{:S(2)}) copy-start(bf16[4,384,1024]{2,1,0:T(8,128)(2,1)} %param.15) | copy-start | bytes 9437188
  8.0 45.8 %copy-start.2 = (bf16[128,1024]{1,0:T(8,128)(2,1)S(1)}, bf16[128,1024]{1,0:T(8,128)(2,1)}, u32[]{:S(2)}) copy-start(bf16[128,1024]{1,0:T(8,128)(2,1)} %param.9) | copy-start | bytes 786436
  61.8 78.2 %copy-start.8 = (bf16[4,384,1024]{2,1,0:T(8,128)(2,1)S(1)}, bf16[4,384,1024]{2,1,0:T(8,128)(2,1)}, u32[]{:S(2)}) copy-start(bf16[4,384,1024]{2,1,0:T(8,128)(2,1)} %param.13) | copy-start | bytes 9437188
  140.0 1.9 copy-start.3
  140.0 3.0 copy-start.9
  143.0 3.5 copy-start.15
  146.5 1.8 copy-start.10
  150.5 8.1 copy-start.14
  150.5 77.1 %all-to-all-start.1 = ((bf16[16,96,1024]{2,1,0:T(8,128)(2,1)}), bf16[16,96,1024]{2,1,0:T(8,128)(2,1)}, u32[]{:S(2)}, u32[]{:S(2)}) async-start(bf16[16,96,1024]{2,1,0:T(8,128)(2,1)} %bitcast.144), calls=%async_computation.1 | async-start | bytes 6291456 | tf_op jit(solution)/shard_map/all_to_all | solution.py:64
  156.6 1009.4 %all-gather.3.cloned.1.call-start = ((), (), s32[]{:S(2)}) async-start(), calls=%async_computation.10 | async-start | bytes 67371008 | tf_op jit(solution)/shard_map/all_gather | solution.py:89
  239.7 1004.2 %reduce-scatter.4.cloned.1.call-start = ((), (), s32[]{:S(2)}) async-start(), calls=%async_computation.7 | async-start | bytes 6684672 | tf_op jit(solution)/shard_map/reduce_scatter | solution.py:131
  254.6 92.9 %copy-start.16 = (f32[4,16,24,384]{3,2,1,0:T(8,128)S(1)}, f32[4,16,24,384]{3,2,1,0:T(8,128)}, u32[]{:S(2)}) copy-start(f32[4,16,24,384]{3,2,1,0:T(8,128)} %copy-done.15) | copy-start | bytes 7077892
  254.6 92.9 %copy-start.17 = (f32[4,16,24,384]{3,2,1,0:T(8,128)S(1)}, f32[4,16,24,384]{3,2,1,0:T(8,128)}, u32[]{:S(2)}) copy-start(f32[4,16,24,384]{3,2,1,0:T(8,128)} %get-tuple-element.18) | copy-start | bytes 7077892
  347.5 3.3 copy-start.6
  347.5 4.4 copy-start.4
  350.8 1.0 copy-start.12
  356.4 1.9 copy-start.5
  356.4 887.5 %reduce-scatter.6.cloned.1.call-start = ((), (), s32[]{:S(2)}) async-start(), calls=%async_computation.8 | async-start | bytes 6684672 | tf_op jit(solution)/shard_map/reduce_scatter | solution.py:132
  364.1 7.4 copy-start.7
  364.1 879.9 %reduce-scatter.8.cloned.1.call-start = ((), (), s32[]{:S(2)}) async-start(), calls=%async_computation.9 | async-start | bytes 6684672 | tf_op jit(solution)/shard_map/reduce_scatter | solution.py:133
  364.3 7.1 copy-start.11
  476.5 5.2 copy-start.13
  1222.4 21.5 %copy-start.1 = (bf16[4,384,1024]{2,1,0:T(8,128)(2,1)S(1)}, bf16[4,384,1024]{2,1,0:T(8,128)(2,1)}, u32[]{:S(2)}) copy-start(bf16[4,384,1024]{2,1,0:T(8,128)(2,1)} %param.15) | copy-start | bytes 9437188
Sparse Core Ops, SparseCore 0:
  239.9 926.0 all-gather.2
Sparse Core Ops, SparseCore 1:
  356.5 110.5 reduce-scatter.3
  471.9 98.9 reduce-scatter.5
  575.7 97.3 reduce-scatter.7
